TPU v7x, 32 devices: a whole 2x2x4 slice. The times are simulated.
32 devices in a mesh: branch: 8 (over z, y), head: 4 (over x, core).
Axes of the slice: x: 2, y: 2, z: 4, core: 2. Of those that a mesh axis runs over, the one named last changes fastest.
Arguments:
- q_latent: bfloat16 [1024, 1536], P(('branch', 'head')), may hold values from -6 to 6
- seg_latent: bfloat16 [1024, 576], P(('branch', 'head')), may hold values from -6 to 6
- trunk_latent: bfloat16 [4096, 576], P(('branch', 'head'))
- visible: int32 [8, 4096], P('branch'), may hold values from 0 to 1, as said below
- w_uq: bfloat16 [1536, 24576], P(None, 'head'), may hold values from -0.15625 to 0.15625
- w_uk: bfloat16 [128, 128, 512], P('head'), may hold values from -0.25 to 0.25
- w_uv: bfloat16 [128, 512, 128], P('head'), may hold values from -0.25 to 0.25
Outputs:
- attended: bfloat16 [1024, 16384], P('branch', 'head')
Inputs may be any that keep to these rules, and one draw needn't show every extreme that they name: `visible`: every branch sees the trunk rows 0 to 1023, then exactly one of four runs of consecutive rows that cover rows 1024 to 3071, and one of eight runs covering the last quarter; the run of the last quarter is one of two children of the branch's run of the middle half. Runs have random lengths and may be empty.
All inputs are finite; a program needn't handle non-finite values.
Results may differ from a plain program's by a relative error of at most 0.009.
The roundings to bfloat16 on the way count: a program that leaves them out, or rounds other values in their place, can miss the bound.
Values may be sent and summed in bfloat16 or wider, within the bound.
No kernel may reach another device: no remote copies, remote signals or barrier semaphores. Data moves between devices by JAX's collectives and lax.ppermute only.
A program may use at most 128 MiB of HBM per device.

v0:
```python
import math

import jax
import jax.numpy as jnp
from jax import lax
from jax.sharding import PartitionSpec as P


def rotate(values, positions):
    half = values.shape[-1] // 2
    freq = 10000.0 ** (-2.0 * jnp.arange(half, dtype=jnp.float32) / values.shape[-1])
    angle = positions.astype(jnp.float32)[:, None, None] * freq[None, None, :]
    first = values[..., :half]
    second = values[..., half:]
    cosine = jnp.cos(angle)
    sine = jnp.sin(angle)
    return jnp.concatenate(
        [first * cosine - second * sine, first * sine + second * cosine], axis=-1
    )


def absorb(carry, query, keys, allowed, scale):
    peak_old, total_old, summed_old = carry
    scores = jnp.einsum("shc,kc->shk", query, keys, preferred_element_type=jnp.float32) * scale
    scores = jnp.where(allowed[:, None, :], scores, -1e30)
    peak_new = jnp.maximum(peak_old, jnp.max(scores, axis=-1))
    factor = jnp.exp(peak_old - peak_new)
    weights = jnp.where(allowed[:, None, :], jnp.exp(scores - peak_new[..., None]), 0.0)
    total_new = total_old * factor + jnp.sum(weights, axis=-1)
    summed_part = jnp.einsum(
        "shk,kc->shc",
        weights.astype(jnp.bfloat16),
        keys[:, : summed_old.shape[-1]],
        preferred_element_type=jnp.float32,
    )
    return (peak_new, total_new, summed_old * factor[..., None] + summed_part)


def shards(q_latent, seg_latent, trunk_latent, visible, w_uq, w_uk, w_uv):
    heads_here = w_uk.shape[0]
    nope_dim = w_uk.shape[1]
    latent_dim = w_uk.shape[2]
    rope_dim = w_uq.shape[1] // heads_here - nope_dim
    scale = 1.0 / (nope_dim + rope_dim) ** 0.5
    q_rows, seg_rows = (
        lax.all_gather(q_latent, "head", axis=0, tiled=True),
        lax.all_gather(seg_latent, "head", axis=0, tiled=True),
    )
    seg_len = q_rows.shape[0]
    seen = visible[0]
    depth = jnp.sum(seen)
    positions = depth + jnp.arange(seg_len, dtype=jnp.int32)
    q_full = jnp.dot(q_rows, w_uq, preferred_element_type=jnp.float32).reshape(
        seg_len, heads_here, nope_dim + rope_dim
    )
    q_nope = q_full[..., :nope_dim].astype(jnp.bfloat16)
    q_rope = rotate(q_full[..., nope_dim:], positions).astype(jnp.bfloat16)
    q_abs = jnp.einsum("shn,hnk->shk", q_nope, w_uk, preferred_element_type=jnp.float32).astype(
        jnp.bfloat16
    )
    query = jnp.concatenate([q_abs, q_rope], axis=-1)
    causal = (
        jnp.arange(seg_len, dtype=jnp.int32)[None, :]
        <= jnp.arange(seg_len, dtype=jnp.int32)[:, None]
    )
    start_carry = (
        jnp.full((seg_len, heads_here), -1e30, jnp.float32),
        jnp.zeros((seg_len, heads_here), jnp.float32),
        jnp.zeros((seg_len, heads_here, latent_dim), jnp.float32),
    )
    carry = absorb(start_carry, query, seg_rows, causal, scale)

    def take_piece(state, piece, start):
        marks = lax.dynamic_slice_in_dim(seen, start, piece.shape[0], 0) > 0
        allowed = jnp.broadcast_to(marks[None, :], (seg_len, piece.shape[0]))
        return absorb(state, query, piece, allowed, scale)

    whole_trunk = lax.all_gather(trunk_latent, ("branch", "head"), axis=0, tiled=True)
    trunk_rows = whole_trunk.shape[0]
    block_rows = math.gcd(trunk_rows, 512)

    def step_block(index, state):
        begin = (index * block_rows).astype(jnp.int32)
        piece = lax.dynamic_slice_in_dim(whole_trunk, begin, block_rows, 0)
        return take_piece(state, piece, begin)

    carry = lax.fori_loop(0, trunk_rows // block_rows, step_block, carry)
    attend = (carry[2] / carry[1][..., None]).astype(jnp.bfloat16)
    result = jnp.einsum("shc,hcv->shv", attend, w_uv, preferred_element_type=jnp.float32)
    return result.astype(jnp.bfloat16).reshape(seg_len, heads_here * w_uv.shape[2])


def solution(mesh):
    placed = (
        P(("branch", "head"), None),
        P(("branch", "head"), None),
        P(("branch", "head"), None),
        P("branch", None),
        P(None, "head"),
        P("head", None, None),
        P("head", None, None),
    )
    return jax.shard_map(
        shards, mesh=mesh, in_specs=placed, out_specs=P("branch", "head"), check_vma=False
    )
```

profile of v0, /device:TPU:21, one launch (start us, length us, event | category | flops | bytes accessed | tf_op | source)
XLA Modules:
  0.0 248.6 jit_solution(5084884142627292505)
XLA Ops:
  7.3 1.4 reduce_sum.31
  8.7 7.2 %all_gather.9 = bf16[128,1536]{1,0:T(8,128)(2,1)S(1)} all-gather(bf16[32,1536]{1,0:T(8,128)(2,1)} %param.9), channel_id=1, replica_groups=mesh['branch'=8,'head'=4] {'head'}, dimensions={0}, use_global_device_ids=true | all-gather | bytes 491520 | tf_op jit(solution)/shard_map/all_gather | solution.py:46
  15.9 11.3 %fusion.40 = f32[128,6144]{0,1:T(8,128)S(1)} fusion(bf16[128,1536]{1,0:T(8,128)(2,1)S(1)} %all_gather.9, bf16[1536,6144]{1,0:T(8,128)(2,1)} %param.13), kind=kOutput, calls=%fused_computation.61 | convolution fusion | flops 2415919104 | bytes 22413312 | tf_op jit(solution)/shard_map/dot_general | solution.py:53
  28.2 3.0 %copy.48 = f32[128,32,32]{2,0,1:T(8,128)} copy(f32[128,32,32]{0,2,1:T(8,128)} %get-tuple-element.173) | data formatting | bytes 1048576
  31.2 3.0 %copy.49 = f32[128,32,32]{2,0,1:T(8,128)} copy(f32[128,32,32]{0,2,1:T(8,128)} %get-tuple-element.174) | data formatting | bytes 1048576
  35.3 3.0 %subtract_convert_fusion = (bf16[128,32,32]{2,0,1:T(8,128)(2,1)S(1)}, bf16[128,32,32]{2,0,1:T(8,128)(2,1)S(1)}) fusion(f32[128,32,32]{2,0,1:T(8,128)} %copy.49, f32[128,32,32]{2,0,1:T(8,128)} %copy.48, f32[128,32]{1,0:T(8,128)S(1)} %get-tuple-element.178, f32[128,32]{1,0:T(8,128)S(1)} %get-tuple-element.177), kind=kLoop, calls=%fused_computation.36 | loop fusion | flops 1048576 | bytes 1605632 | tf_op jit(solution)/shard_map/convert
  38.2 1.3 convert_bitcast_fusion
  39.5 3.4 %pad_maximum_fusion = bf16[128,32,576]{2,0,1:T(8,128)(2,1)} fusion(bf16[128,32,32]{2,0,1:T(8,128)(2,1)S(1)} %get-tuple-element.172, bf16[128,32,32]{2,0,1:T(8,128)(2,1)S(1)} %get-tuple-element.171, bf16[128,32,512]{2,0,1:T(8,128)(2,1)S(1)} %convert_bitcast_fusion), kind=kLoop, calls=%fused_computation.28 | loop fusion | flops 14155776 | bytes 9437184 | tf_op jit(solution)/shard_map/concatenate | solution.py:61
  42.9 7.6 %copy.37 = bf16[128,32,576]{0,2,1:T(8,128)(2,1)} copy(bf16[128,32,576]{2,0,1:T(8,128)(2,1)} %pad_maximum_fusion) | data formatting | bytes 9437184 | tf_op jit(solution)/shard_map/while | solution.py:87
  50.5 5.5 %all_gather.10 = bf16[128,576]{1,0:T(8,128)(2,1)S(1)} all-gather(bf16[32,576]{1,0:T(8,128)(2,1)S(1)} %copy-done.2), channel_id=1, replica_groups=mesh['branch'=8,'head'=4] {'head'}, dimensions={0}, use_global_device_ids=true | all-gather | bytes 184320 | tf_op jit(solution)/shard_map/all_gather | solution.py:47
  56.0 4.3 %fusion.23 = (f32[128,32]{0,1:T(8,128)S(1)}, f32[128,32,128]{0,2,1:T(8,128)S(1)}) fusion(pred[128,128]{0,1:T(8,128)(4,1)S(1)} %iota_compare_fusion, bf16[128,32,576]{2,0,1:T(8,128)(2,1)} %pad_maximum_fusion, bf16[128,576]{1,0:T(8,128)(2,1)S(1)} %all_gather.10), kind=kOutput, calls=%fused_computation.37 | convolution fusion | flops 605548544 | bytes 6995968 | tf_op jit(solution)/shard_map/shc,kc->shk/dot_general | solution.py:24
  61.0 4.2 %broadcast_add_fusion = f32[128,32,512]{2,0,1:T(8,128)} fusion(f32[128,32]{0,1:T(8,128)S(1)} %get-tuple-element.175, f32[128,32,128]{0,2,1:T(8,128)S(1)} %get-tuple-element.180, f32[128,32]{0,1:T(8,128)S(1)} %broadcast_maximum_fusion, pred[128,128]{0,1:T(8,128)(4,1)S(1)} %iota_compare_fusion, bf16[128,576]{1,0:T(8,128)(2,1)S(1)} %all_gather.10), kind=kOutput, calls=%fused_computation.29 | convolution fusion | flops 541589504 | bytes 10665984 | tf_op jit(solution)/shard_map/shk,kc->shc/dot_general | solution.py:30
  65.2 14.4 %all-gather.2.cloned.1.call-done = bf16[4096,576]{0,1:T(8,128)(2,1)} async-done(((bf16[128,576]{0,1:T(8,128)(2,1)}), bf16[4096,576]{0,1:T(8,128)(2,1)}) %all-gather.2.cloned.1.call-update) | async-done | bytes 4718608 | tf_op jit(solution)/shard_map/all_gather | solution.py:78
  79.6 154.3 %while.17 = (s32[]{:T(128)}, f32[128,32]{0,1:T(8,128)S(1)}, f32[128,32]{0,1:T(8,128)S(1)}, f32[128,32,512]{2,0,1:T(8,128)}, s32[4096]{0:T(1024)}, /*index=5*/bf1...) while((s32[]{:T(128)}, f32[128,32]{0,1:T(8,128)S(1)}, ...), condition=%wide.region_6.7_spmd, body=%wide.region_3.6_spmd.sunk | while | flops 4594868736 | bytes 106762984 | solution.py:87
  80.5 6.1 %bitcast_reduce_fusion.2 = (f32[128,32]{0,1:T(8,128)S(1)}, f32[512,128,32]{1,0,2:T(8,128)S(1)}) fusion(pred[512]{0:T(512)(128)(4,1)S(1)} %dynamic-slice_compare_fusion.2, bf16[128,32,576]{0,2,1:T(8,128)(2,1)} %get-tuple-element.260, bf16[4096,576]{0,1:T(8,128)(2,1)} %get-tuple-element.259, s32[]{:T(128)S(6)} %select_n.82), kind=kOutput, calls=%fused_computation.1.clone.1 | convolution fusion | flops 2422206464 | bytes 13713924 | tf_op jit(solution)/shard_map/while/body/eval_jaxpr/shc,kc->shk/dot_general | solution.py:24
  86.6 2.4 fusion.52
  89.1 6.6 %multiply_add_fusion.5 = f32[128,32,512]{2,0,1:T(8,128)S(1)} fusion(f32[128,32,512]{2,0,1:T(8,128)S(1)} %bitcast.56, f32[128,32]{0,1:T(8,128)S(1)} %get-tuple-element.231, f32[512,128,32]{1,0,2:T(8,128)S(1)} %get-tuple-element.229, f32[128,32]{0,1:T(8,128)S(1)} %max.8, pred[512]{0:T(512)(128)(4,1)S(1)} %dynamic-slice_compare_fusion.2, ...), kind=kOutput, calls=%fused_computation.4.clone.1 | convolution fusion | flops 2162163712 | bytes 25723908 | tf_op jit(solution)/shard_map/while/body/eval_jaxpr/shk,kc->shc/dot_general | solution.py:30
  95.7 3.2 %copy-done = f32[128,32,512]{2,0,1:T(8,128)} copy-done((f32[128,32,512]{2,0,1:T(8,128)}, f32[128,32,512]{2,0,1:T(8,128)S(1)}, u32[]{:S(2)}) %copy-start) | copy-done | bytes 8388632 | tf_op jit(solution)/shard_map/while
  99.8 6.1 %bitcast_reduce_fusion.2 = (f32[128,32]{0,1:T(8,128)S(1)}, f32[512,128,32]{1,0,2:T(8,128)S(1)}) fusion(pred[512]{0:T(512)(128)(4,1)S(1)} %dynamic-slice_compare_fusion.2, bf16[128,32,576]{0,2,1:T(8,128)(2,1)} %get-tuple-element.260, bf16[4096,576]{0,1:T(8,128)(2,1)} %get-tuple-element.259, s32[]{:T(128)S(6)} %select_n.82), kind=kOutput, calls=%fused_computation.1.clone.1 | convolution fusion | flops 2422206464 | bytes 13713924 | tf_op jit(solution)/shard_map/while/body/eval_jaxpr/shc,kc->shk/dot_general | solution.py:24
  105.9 2.4 fusion.52
  108.3 6.6 %multiply_add_fusion.5 = f32[128,32,512]{2,0,1:T(8,128)S(1)} fusion(f32[128,32,512]{2,0,1:T(8,128)S(1)} %bitcast.56, f32[128,32]{0,1:T(8,128)S(1)} %get-tuple-element.231, f32[512,128,32]{1,0,2:T(8,128)S(1)} %get-tuple-element.229, f32[128,32]{0,1:T(8,128)S(1)} %max.8, pred[512]{0:T(512)(128)(4,1)S(1)} %dynamic-slice_compare_fusion.2, ...), kind=kOutput, calls=%fused_computation.4.clone.1 | convolution fusion | flops 2162163712 | bytes 25723908 | tf_op jit(solution)/shard_map/while/body/eval_jaxpr/shk,kc->shc/dot_general | solution.py:30
  115.0 3.2 %copy-done = f32[128,32,512]{2,0,1:T(8,128)} copy-done((f32[128,32,512]{2,0,1:T(8,128)}, f32[128,32,512]{2,0,1:T(8,128)S(1)}, u32[]{:S(2)}) %copy-start) | copy-done | bytes 8388632 | tf_op jit(solution)/shard_map/while
  119.1 6.1 %bitcast_reduce_fusion.2 = (f32[128,32]{0,1:T(8,128)S(1)}, f32[512,128,32]{1,0,2:T(8,128)S(1)}) fusion(pred[512]{0:T(512)(128)(4,1)S(1)} %dynamic-slice_compare_fusion.2, bf16[128,32,576]{0,2,1:T(8,128)(2,1)} %get-tuple-element.260, bf16[4096,576]{0,1:T(8,128)(2,1)} %get-tuple-element.259, s32[]{:T(128)S(6)} %select_n.82), kind=kOutput, calls=%fused_computation.1.clone.1 | convolution fusion | flops 2422206464 | bytes 13713924 | tf_op jit(solution)/shard_map/while/body/eval_jaxpr/shc,kc->shk/dot_general | solution.py:24
  125.2 2.4 fusion.52
  127.6 6.6 %multiply_add_fusion.5 = f32[128,32,512]{2,0,1:T(8,128)S(1)} fusion(f32[128,32,512]{2,0,1:T(8,128)S(1)} %bitcast.56, f32[128,32]{0,1:T(8,128)S(1)} %get-tuple-element.231, f32[512,128,32]{1,0,2:T(8,128)S(1)} %get-tuple-element.229, f32[128,32]{0,1:T(8,128)S(1)} %max.8, pred[512]{0:T(512)(128)(4,1)S(1)} %dynamic-slice_compare_fusion.2, ...), kind=kOutput, calls=%fused_computation.4.clone.1 | convolution fusion | flops 2162163712 | bytes 25723908 | tf_op jit(solution)/shard_map/while/body/eval_jaxpr/shk,kc->shc/dot_general | solution.py:30
  134.3 3.2 %copy-done = f32[128,32,512]{2,0,1:T(8,128)} copy-done((f32[128,32,512]{2,0,1:T(8,128)}, f32[128,32,512]{2,0,1:T(8,128)S(1)}, u32[]{:S(2)}) %copy-start) | copy-done | bytes 8388632 | tf_op jit(solution)/shard_map/while
  138.4 6.1 %bitcast_reduce_fusion.2 = (f32[128,32]{0,1:T(8,128)S(1)}, f32[512,128,32]{1,0,2:T(8,128)S(1)}) fusion(pred[512]{0:T(512)(128)(4,1)S(1)} %dynamic-slice_compare_fusion.2, bf16[128,32,576]{0,2,1:T(8,128)(2,1)} %get-tuple-element.260, bf16[4096,576]{0,1:T(8,128)(2,1)} %get-tuple-element.259, s32[]{:T(128)S(6)} %select_n.82), kind=kOutput, calls=%fused_computation.1.clone.1 | convolution fusion | flops 2422206464 | bytes 13713924 | tf_op jit(solution)/shard_map/while/body/eval_jaxpr/shc,kc->shk/dot_general | solution.py:24
  144.5 2.4 fusion.52
  146.9 6.6 %multiply_add_fusion.5 = f32[128,32,512]{2,0,1:T(8,128)S(1)} fusion(f32[128,32,512]{2,0,1:T(8,128)S(1)} %bitcast.56, f32[128,32]{0,1:T(8,128)S(1)} %get-tuple-element.231, f32[512,128,32]{1,0,2:T(8,128)S(1)} %get-tuple-element.229, f32[128,32]{0,1:T(8,128)S(1)} %max.8, pred[512]{0:T(512)(128)(4,1)S(1)} %dynamic-slice_compare_fusion.2, ...), kind=kOutput, calls=%fused_computation.4.clone.1 | convolution fusion | flops 2162163712 | bytes 25723908 | tf_op jit(solution)/shard_map/while/body/eval_jaxpr/shk,kc->shc/dot_general | solution.py:30
  153.6 3.2 %copy-done = f32[128,32,512]{2,0,1:T(8,128)} copy-done((f32[128,32,512]{2,0,1:T(8,128)}, f32[128,32,512]{2,0,1:T(8,128)S(1)}, u32[]{:S(2)}) %copy-start) | copy-done | bytes 8388632 | tf_op jit(solution)/shard_map/while
  157.7 6.1 %bitcast_reduce_fusion.2 = (f32[128,32]{0,1:T(8,128)S(1)}, f32[512,128,32]{1,0,2:T(8,128)S(1)}) fusion(pred[512]{0:T(512)(128)(4,1)S(1)} %dynamic-slice_compare_fusion.2, bf16[128,32,576]{0,2,1:T(8,128)(2,1)} %get-tuple-element.260, bf16[4096,576]{0,1:T(8,128)(2,1)} %get-tuple-element.259, s32[]{:T(128)S(6)} %select_n.82), kind=kOutput, calls=%fused_computation.1.clone.1 | convolution fusion | flops 2422206464 | bytes 13713924 | tf_op jit(solution)/shard_map/while/body/eval_jaxpr/shc,kc->shk/dot_general | solution.py:24
  163.8 2.4 fusion.52
  166.2 6.6 %multiply_add_fusion.5 = f32[128,32,512]{2,0,1:T(8,128)S(1)} fusion(f32[128,32,512]{2,0,1:T(8,128)S(1)} %bitcast.56, f32[128,32]{0,1:T(8,128)S(1)} %get-tuple-element.231, f32[512,128,32]{1,0,2:T(8,128)S(1)} %get-tuple-element.229, f32[128,32]{0,1:T(8,128)S(1)} %max.8, pred[512]{0:T(512)(128)(4,1)S(1)} %dynamic-slice_compare_fusion.2, ...), kind=kOutput, calls=%fused_computation.4.clone.1 | convolution fusion | flops 2162163712 | bytes 25723908 | tf_op jit(solution)/shard_map/while/body/eval_jaxpr/shk,kc->shc/dot_general | solution.py:30
  172.8 3.2 %copy-done = f32[128,32,512]{2,0,1:T(8,128)} copy-done((f32[128,32,512]{2,0,1:T(8,128)}, f32[128,32,512]{2,0,1:T(8,128)S(1)}, u32[]{:S(2)}) %copy-start) | copy-done | bytes 8388632 | tf_op jit(solution)/shard_map/while
  177.0 6.1 %bitcast_reduce_fusion.2 = (f32[128,32]{0,1:T(8,128)S(1)}, f32[512,128,32]{1,0,2:T(8,128)S(1)}) fusion(pred[512]{0:T(512)(128)(4,1)S(1)} %dynamic-slice_compare_fusion.2, bf16[128,32,576]{0,2,1:T(8,128)(2,1)} %get-tuple-element.260, bf16[4096,576]{0,1:T(8,128)(2,1)} %get-tuple-element.259, s32[]{:T(128)S(6)} %select_n.82), kind=kOutput, calls=%fused_computation.1.clone.1 | convolution fusion | flops 2422206464 | bytes 13713924 | tf_op jit(solution)/shard_map/while/body/eval_jaxpr/shc,kc->shk/dot_general | solution.py:24
  183.0 2.4 fusion.52
  185.5 6.6 %multiply_add_fusion.5 = f32[128,32,512]{2,0,1:T(8,128)S(1)} fusion(f32[128,32,512]{2,0,1:T(8,128)S(1)} %bitcast.56, f32[128,32]{0,1:T(8,128)S(1)} %get-tuple-element.231, f32[512,128,32]{1,0,2:T(8,128)S(1)} %get-tuple-element.229, f32[128,32]{0,1:T(8,128)S(1)} %max.8, pred[512]{0:T(512)(128)(4,1)S(1)} %dynamic-slice_compare_fusion.2, ...), kind=kOutput, calls=%fused_computation.4.clone.1 | convolution fusion | flops 2162163712 | bytes 25723908 | tf_op jit(solution)/shard_map/while/body/eval_jaxpr/shk,kc->shc/dot_general | solution.py:30
  192.1 3.2 %copy-done = f32[128,32,512]{2,0,1:T(8,128)} copy-done((f32[128,32,512]{2,0,1:T(8,128)}, f32[128,32,512]{2,0,1:T(8,128)S(1)}, u32[]{:S(2)}) %copy-start) | copy-done | bytes 8388632 | tf_op jit(solution)/shard_map/while
  196.2 6.1 %bitcast_reduce_fusion.2 = (f32[128,32]{0,1:T(8,128)S(1)}, f32[512,128,32]{1,0,2:T(8,128)S(1)}) fusion(pred[512]{0:T(512)(128)(4,1)S(1)} %dynamic-slice_compare_fusion.2, bf16[128,32,576]{0,2,1:T(8,128)(2,1)} %get-tuple-element.260, bf16[4096,576]{0,1:T(8,128)(2,1)} %get-tuple-element.259, s32[]{:T(128)S(6)} %select_n.82), kind=kOutput, calls=%fused_computation.1.clone.1 | convolution fusion | flops 2422206464 | bytes 13713924 | tf_op jit(solution)/shard_map/while/body/eval_jaxpr/shc,kc->shk/dot_general | solution.py:24
  202.3 2.4 fusion.52
  204.8 6.6 %multiply_add_fusion.5 = f32[128,32,512]{2,0,1:T(8,128)S(1)} fusion(f32[128,32,512]{2,0,1:T(8,128)S(1)} %bitcast.56, f32[128,32]{0,1:T(8,128)S(1)} %get-tuple-element.231, f32[512,128,32]{1,0,2:T(8,128)S(1)} %get-tuple-element.229, f32[128,32]{0,1:T(8,128)S(1)} %max.8, pred[512]{0:T(512)(128)(4,1)S(1)} %dynamic-slice_compare_fusion.2, ...), kind=kOutput, calls=%fused_computation.4.clone.1 | convolution fusion | flops 2162163712 | bytes 25723908 | tf_op jit(solution)/shard_map/while/body/eval_jaxpr/shk,kc->shc/dot_general | solution.py:30
  211.4 3.2 %copy-done = f32[128,32,512]{2,0,1:T(8,128)} copy-done((f32[128,32,512]{2,0,1:T(8,128)}, f32[128,32,512]{2,0,1:T(8,128)S(1)}, u32[]{:S(2)}) %copy-start) | copy-done | bytes 8388632 | tf_op jit(solution)/shard_map/while
  215.5 6.1 %bitcast_reduce_fusion.2 = (f32[128,32]{0,1:T(8,128)S(1)}, f32[512,128,32]{1,0,2:T(8,128)S(1)}) fusion(pred[512]{0:T(512)(128)(4,1)S(1)} %dynamic-slice_compare_fusion.2, bf16[128,32,576]{0,2,1:T(8,128)(2,1)} %get-tuple-element.260, bf16[4096,576]{0,1:T(8,128)(2,1)} %get-tuple-element.259, s32[]{:T(128)S(6)} %select_n.82), kind=kOutput, calls=%fused_computation.1.clone.1 | convolution fusion | flops 2422206464 | bytes 13713924 | tf_op jit(solution)/shard_map/while/body/eval_jaxpr/shc,kc->shk/dot_general | solution.py:24
  221.6 2.4 fusion.52
  224.1 6.6 %multiply_add_fusion.5 = f32[128,32,512]{2,0,1:T(8,128)S(1)} fusion(f32[128,32,512]{2,0,1:T(8,128)S(1)} %bitcast.56, f32[128,32]{0,1:T(8,128)S(1)} %get-tuple-element.231, f32[512,128,32]{1,0,2:T(8,128)S(1)} %get-tuple-element.229, f32[128,32]{0,1:T(8,128)S(1)} %max.8, pred[512]{0:T(512)(128)(4,1)S(1)} %dynamic-slice_compare_fusion.2, ...), kind=kOutput, calls=%fused_computation.4.clone.1 | convolution fusion | flops 2162163712 | bytes 25723908 | tf_op jit(solution)/shard_map/while/body/eval_jaxpr/shk,kc->shc/dot_general | solution.py:30
  230.7 3.2 %copy-done = f32[128,32,512]{2,0,1:T(8,128)} copy-done((f32[128,32,512]{2,0,1:T(8,128)}, f32[128,32,512]{2,0,1:T(8,128)S(1)}, u32[]{:S(2)}) %copy-start) | copy-done | bytes 8388632 | tf_op jit(solution)/shard_map/while
  233.9 6.5 %fusion.24 = bf16[32,128,128]{1,2,0:T(8,128)(2,1)S(1)} fusion(bf16[32,512,128]{2,1,0:T(8,128)(2,1)} %param.15, f32[128,32,512]{2,0,1:T(8,128)} %get-tuple-element.130, f32[128,32]{0,1:T(8,128)S(1)} %get-tuple-element.131), kind=kOutput, calls=%fused_computation.38 | convolution fusion | flops 541589504 | bytes 13647872 | tf_op jit(solution)/shard_map/shc,hcv->shv/dot_general | solution.py:89
  240.4 1.3 copy.39
  (94 shorter events, 11.0 us)
Async XLA Ops:
  6.5 73.1 %all-gather.2.cloned.1.call-start = ((), (), s32[]{:S(2)}) async-start(), calls=%async_computation | async-start | bytes 4866048 | tf_op jit(solution)/shard_map/all_gather | solution.py:78
  34.1 4.1 %copy-start.1 = (bf16[32,128,512]{2,1,0:T(8,128)(2,1)S(1)}, bf16[32,128,512]{2,1,0:T(8,128)(2,1)}, u32[]{:S(2)}) copy-start(bf16[32,128,512]{2,1,0:T(8,128)(2,1)} %param.14) | copy-start | bytes 12582916
  42.9 7.6 %copy-start.2 = (bf16[32,576]{1,0:T(8,128)(2,1)S(1)}, bf16[32,576]{1,0:T(8,128)(2,1)}, u32[]{:S(2)}) copy-start(bf16[32,576]{1,0:T(8,128)(2,1)} %param.10) | copy-start | bytes 110596
  79.6 9.4 %slice-start = ((s8[8388608]{0:T(1024)(128)(4,1)}), s8[4194304]{0:T(1024)(128)(4,1)S(1)}, s32[]{:S(2)}) async-start(s8[8388608]{0:T(1024)(128)(4,1)} %bitcast.55), calls=%async_computation.1 | async-start | bytes 8388608 | tf_op jit(solution)/shard_map/while
  80.5 8.5 %slice-start.1 = ((s8[8388608]{0:T(1024)(128)(4,1)}), s8[4194304]{0:T(1024)(128)(4,1)S(1)}, s32[]{:S(2)}) async-start(s8[8388608]{0:T(1024)(128)(4,1)} %bitcast.55), calls=%async_computation.2 | async-start | bytes 8388608 | tf_op jit(solution)/shard_map/while
  95.7 3.2 %copy-start = (f32[128,32,512]{2,0,1:T(8,128)}, f32[128,32,512]{2,0,1:T(8,128)S(1)}, u32[]{:S(2)}) copy-start(f32[128,32,512]{2,0,1:T(8,128)S(1)} %multiply_add_fusion.5) | copy-start | bytes 25165828 | tf_op jit(solution)/shard_map/while
  98.9 9.4 %slice-start = ((s8[8388608]{0:T(1024)(128)(4,1)}), s8[4194304]{0:T(1024)(128)(4,1)S(1)}, s32[]{:S(2)}) async-start(s8[8388608]{0:T(1024)(128)(4,1)} %bitcast.55), calls=%async_computation.1 | async-start | bytes 8388608 | tf_op jit(solution)/shard_map/while
  99.8 8.5 %slice-start.1 = ((s8[8388608]{0:T(1024)(128)(4,1)}), s8[4194304]{0:T(1024)(128)(4,1)S(1)}, s32[]{:S(2)}) async-start(s8[8388608]{0:T(1024)(128)(4,1)} %bitcast.55), calls=%async_computation.2 | async-start | bytes 8388608 | tf_op jit(solution)/shard_map/while
  115.0 3.2 %copy-start = (f32[128,32,512]{2,0,1:T(8,128)}, f32[128,32,512]{2,0,1:T(8,128)S(1)}, u32[]{:S(2)}) copy-start(f32[128,32,512]{2,0,1:T(8,128)S(1)} %multiply_add_fusion.5) | copy-start | bytes 25165828 | tf_op jit(solution)/shard_map/while
  118.2 9.4 %slice-start = ((s8[8388608]{0:T(1024)(128)(4,1)}), s8[4194304]{0:T(1024)(128)(4,1)S(1)}, s32[]{:S(2)}) async-start(s8[8388608]{0:T(1024)(128)(4,1)} %bitcast.55), calls=%async_computation.1 | async-start | bytes 8388608 | tf_op jit(solution)/shard_map/while
  119.1 8.5 %slice-start.1 = ((s8[8388608]{0:T(1024)(128)(4,1)}), s8[4194304]{0:T(1024)(128)(4,1)S(1)}, s32[]{:S(2)}) async-start(s8[8388608]{0:T(1024)(128)(4,1)} %bitcast.55), calls=%async_computation.2 | async-start | bytes 8388608 | tf_op jit(solution)/shard_map/while
  134.3 3.2 %copy-start = (f32[128,32,512]{2,0,1:T(8,128)}, f32[128,32,512]{2,0,1:T(8,128)S(1)}, u32[]{:S(2)}) copy-start(f32[128,32,512]{2,0,1:T(8,128)S(1)} %multiply_add_fusion.5) | copy-start | bytes 25165828 | tf_op jit(solution)/shard_map/while
  137.5 9.4 %slice-start = ((s8[8388608]{0:T(1024)(128)(4,1)}), s8[4194304]{0:T(1024)(128)(4,1)S(1)}, s32[]{:S(2)}) async-start(s8[8388608]{0:T(1024)(128)(4,1)} %bitcast.55), calls=%async_computation.1 | async-start | bytes 8388608 | tf_op jit(solution)/shard_map/while
  138.4 8.5 %slice-start.1 = ((s8[8388608]{0:T(1024)(128)(4,1)}), s8[4194304]{0:T(1024)(128)(4,1)S(1)}, s32[]{:S(2)}) async-start(s8[8388608]{0:T(1024)(128)(4,1)} %bitcast.55), calls=%async_computation.2 | async-start | bytes 8388608 | tf_op jit(solution)/shard_map/while
  153.5 3.2 %copy-start = (f32[128,32,512]{2,0,1:T(8,128)}, f32[128,32,512]{2,0,1:T(8,128)S(1)}, u32[]{:S(2)}) copy-start(f32[128,32,512]{2,0,1:T(8,128)S(1)} %multiply_add_fusion.5) | copy-start | bytes 25165828 | tf_op jit(solution)/shard_map/while
  156.8 9.4 %slice-start = ((s8[8388608]{0:T(1024)(128)(4,1)}), s8[4194304]{0:T(1024)(128)(4,1)S(1)}, s32[]{:S(2)}) async-start(s8[8388608]{0:T(1024)(128)(4,1)} %bitcast.55), calls=%async_computation.1 | async-start | bytes 8388608 | tf_op jit(solution)/shard_map/while
  157.7 8.5 %slice-start.1 = ((s8[8388608]{0:T(1024)(128)(4,1)}), s8[4194304]{0:T(1024)(128)(4,1)S(1)}, s32[]{:S(2)}) async-start(s8[8388608]{0:T(1024)(128)(4,1)} %bitcast.55), calls=%async_computation.2 | async-start | bytes 8388608 | tf_op jit(solution)/shard_map/while
  172.8 3.2 %copy-start = (f32[128,32,512]{2,0,1:T(8,128)}, f32[128,32,512]{2,0,1:T(8,128)S(1)}, u32[]{:S(2)}) copy-start(f32[128,32,512]{2,0,1:T(8,128)S(1)} %multiply_add_fusion.5) | copy-start | bytes 25165828 | tf_op jit(solution)/shard_map/while
  176.0 9.4 %slice-start = ((s8[8388608]{0:T(1024)(128)(4,1)}), s8[4194304]{0:T(1024)(128)(4,1)S(1)}, s32[]{:S(2)}) async-start(s8[8388608]{0:T(1024)(128)(4,1)} %bitcast.55), calls=%async_computation.1 | async-start | bytes 8388608 | tf_op jit(solution)/shard_map/while
  177.0 8.5 %slice-start.1 = ((s8[8388608]{0:T(1024)(128)(4,1)}), s8[4194304]{0:T(1024)(128)(4,1)S(1)}, s32[]{:S(2)}) async-start(s8[8388608]{0:T(1024)(128)(4,1)} %bitcast.55), calls=%async_computation.2 | async-start | bytes 8388608 | tf_op jit(solution)/shard_map/while
  192.1 3.2 %copy-start = (f32[128,32,512]{2,0,1:T(8,128)}, f32[128,32,512]{2,0,1:T(8,128)S(1)}, u32[]{:S(2)}) copy-start(f32[128,32,512]{2,0,1:T(8,128)S(1)} %multiply_add_fusion.5) | copy-start | bytes 25165828 | tf_op jit(solution)/shard_map/while
  195.3 9.4 %slice-start = ((s8[8388608]{0:T(1024)(128)(4,1)}), s8[4194304]{0:T(1024)(128)(4,1)S(1)}, s32[]{:S(2)}) async-start(s8[8388608]{0:T(1024)(128)(4,1)} %bitcast.55), calls=%async_computation.1 | async-start | bytes 8388608 | tf_op jit(solution)/shard_map/while
  196.2 8.5 %slice-start.1 = ((s8[8388608]{0:T(1024)(128)(4,1)}), s8[4194304]{0:T(1024)(128)(4,1)S(1)}, s32[]{:S(2)}) async-start(s8[8388608]{0:T(1024)(128)(4,1)} %bitcast.55), calls=%async_computation.2 | async-start | bytes 8388608 | tf_op jit(solution)/shard_map/while
  211.4 3.2 %copy-start = (f32[128,32,512]{2,0,1:T(8,128)}, f32[128,32,512]{2,0,1:T(8,128)S(1)}, u32[]{:S(2)}) copy-start(f32[128,32,512]{2,0,1:T(8,128)S(1)} %multiply_add_fusion.5) | copy-start | bytes 25165828 | tf_op jit(solution)/shard_map/while
  214.6 9.4 %slice-start = ((s8[8388608]{0:T(1024)(128)(4,1)}), s8[4194304]{0:T(1024)(128)(4,1)S(1)}, s32[]{:S(2)}) async-start(s8[8388608]{0:T(1024)(128)(4,1)} %bitcast.55), calls=%async_computation.1 | async-start | bytes 8388608 | tf_op jit(solution)/shard_map/while
  215.5 8.5 %slice-start.1 = ((s8[8388608]{0:T(1024)(128)(4,1)}), s8[4194304]{0:T(1024)(128)(4,1)S(1)}, s32[]{:S(2)}) async-start(s8[8388608]{0:T(1024)(128)(4,1)} %bitcast.55), calls=%async_computation.2 | async-start | bytes 8388608 | tf_op jit(solution)/shard_map/while
  230.7 3.2 %copy-start = (f32[128,32,512]{2,0,1:T(8,128)}, f32[128,32,512]{2,0,1:T(8,128)S(1)}, u32[]{:S(2)}) copy-start(f32[128,32,512]{2,0,1:T(8,128)S(1)} %multiply_add_fusion.5) | copy-start | bytes 25165828 | tf_op jit(solution)/shard_map/while
Sparse Core Ops, SparseCore 0:
  10.2 69.3 all-gather.1
where the time goes:
time: 252 us; the launch traced here: 249 us
  matrix products  129 us (51%)
  local copies, waits for them, and re-layouts  41.6 us (17%)
  other arithmetic  36.1 us (14%)
  waiting for transfers between devices  15.1 us (6%)
  between operations  13.5 us (5%)
  blocking collectives  12.7 us (5%)
    dot_general x9, matrix products, absorb(): jnp.einsum('shk,kc->shc', weights.astype(jnp.bfloat16), keys[:, :summed_o...  57.1 us
    dot_general x9, matrix products, absorb(): jnp.einsum('shc,kc->shk', query, keys, preferred_element_type=jnp.float32)  52.8 us
    while x56, local copies, waits for them, and re-layouts  25.7 us
    reduce_sum x9, other arithmetic, absorb(): total_new = total_old * factor + jnp.sum(weights, axis=-1)  19.7 us
    all_gather x1, waiting for transfers between devices, shards(): lax.all_gather(trunk_latent, ('branch', 'head'), axis=0, tiled=True)  14.4 us
    dot_general x1, matrix products, shards(): jnp.dot(q_rows, w_uq, preferred_element_type=jnp.float32)  11.3 us
    while x1, local copies, waits for them, and re-layouts, shards(): carry = lax.fori_loop(0, trunk_rows // block_rows, step_block, carry)  7.58 us
    gt x8, other arithmetic, take_piece(): marks = lax.dynamic_slice_in_dim(seen, start, piece.shape[0], 0) > 0  7.3 us
  transfers between devices with their start and end apart: 1, of which 1 were waited for; matrix products, arithmetic and copies ran while one was open for 18% of the time, Pallas kernels for 0%

commit v1 on v0

v1 whole, which is shorter than its diff:
```python
import functools

import jax
import jax.numpy as jnp
from jax import lax
from jax.experimental import pallas as pl
from jax.experimental.pallas import tpu as pltpu
from jax.sharding import PartitionSpec as P

AXES = ("branch", "head")
BLOCK = 128
HIDDEN = -1e30
LOG2E = 1.4426950408889634
NT = (((1,), (1,)), ((), ()))


def query_kernel(qs_ref, cos_ref, sin_ref, wuq_ref, wuk_ref, out_ref, *, rope):
    group, nope, lat = wuk_ref.shape
    width = nope + rope
    half = rope // 2
    q = jnp.dot(qs_ref[...], wuq_ref[...], preferred_element_type=jnp.float32)
    for g in range(group):
        q_nope = q[:, g * width : g * width + nope].astype(jnp.bfloat16)
        x = q[:, g * width + nope : (g + 1) * width]
        swapped = jnp.concatenate([x[:, half:], x[:, :half]], axis=1)
        q_rope = x * cos_ref[...] + swapped * sin_ref[...]
        q_abs = jnp.dot(q_nope, wuk_ref[g], preferred_element_type=jnp.float32)
        out_ref[g, :, :lat] = q_abs.astype(jnp.bfloat16)
        out_ref[g, :, lat:] = q_rope.astype(jnp.bfloat16)


def make_query(qs, cosine, sine, w_uq, w_uk, group=8):
    seg_len = qs.shape[0]
    rank = w_uq.shape[0]
    heads, nope, lat = w_uk.shape
    width = w_uq.shape[1] // heads
    rope = width - nope
    group = min(group, heads)
    return pl.pallas_call(
        functools.partial(query_kernel, rope=rope),
        grid=(heads // group,),
        in_specs=[
            pl.BlockSpec((seg_len, rank), lambda i: (0, 0)),
            pl.BlockSpec((seg_len, rope), lambda i: (0, 0)),
            pl.BlockSpec((seg_len, rope), lambda i: (0, 0)),
            pl.BlockSpec((rank, group * width), lambda i: (0, i)),
            pl.BlockSpec((group, nope, lat), lambda i: (i, 0, 0)),
        ],
        out_specs=pl.BlockSpec((group, seg_len, lat + rope), lambda i: (i, 0, 0)),
        out_shape=jax.ShapeDtypeStruct((heads, seg_len, lat + rope), jnp.bfloat16),
        compiler_params=pltpu.CompilerParams(vmem_limit_bytes=32 << 20),
        cost_estimate=pl.CostEstimate(
            flops=2 * seg_len * heads * (rank * width + nope * lat),
            bytes_accessed=2 * (w_uq.size + w_uk.size + seg_len * heads * (lat + rope)),
            transcendentals=0,
        ),
        name="query",
    )(qs, cosine, sine, w_uq, w_uk)


def lane_sums(p):
    return functools.reduce(
        jnp.add, [p[:, j : j + 128] for j in range(0, p.shape[1], 128)]
    )


def attend_kernel(
    counts, owners, q_ref, seg_ref, seen_ref, wuv_ref, *rest, pieces, sub, wide, scale
):
    piece_refs, out_ref = rest[:pieces], rest[pieces]
    keys, bias, m_ref, l_ref, acc_ref, meta, sem = rest[pieces + 1 :]
    group, lat, vd = wuv_ref.shape
    s = seg_ref.shape[1]
    blocks = counts.shape[0]
    root = blocks // 4
    factor = scale * LOG2E

    @pl.when(pl.program_id(0) == 0)
    def _():
        def place(i, at):
            meta[i] = at
            return at + (counts[i] > 0).astype(jnp.int32)

        used = lax.fori_loop(0, blocks, place, jnp.int32(1))
        meta[blocks] = used

        def moves(act):
            k = 0
            for ref in piece_refs:
                for j in range(ref.shape[0]):
                    def move(owner, source, ref=ref, j=j):
                        @pl.when(counts[owner] > 0)
                        def _():
                            lane = pl.multiple_of(meta[owner] * BLOCK, BLOCK)
                            act(
                                pltpu.make_async_copy(
                                    source, keys.at[:, pl.ds(lane, BLOCK)], sem
                                )
                            )

                    for t in range(ref.shape[2] // BLOCK):
                        move(owners[k], ref.at[j, :, pl.ds(t * BLOCK, BLOCK)])
                        k += 1

        moves(lambda copy: copy.start())
        keys[:, :BLOCK] = seg_ref[...]
        bias[:, :BLOCK] = jnp.zeros((1, BLOCK), jnp.float32)

        def fill(i, carry):
            @pl.when(counts[i] > 0)
            def _():
                mark = seen_ref[:, pl.ds(pl.multiple_of(i * BLOCK, BLOCK), BLOCK)]
                lane = pl.multiple_of(meta[i] * BLOCK, BLOCK)
                bias[:, pl.ds(lane, BLOCK)] = jnp.where(mark > 0, 0.0, HIDDEN)

            return carry

        lax.fori_loop(0, blocks, fill, 0)
        moves(lambda copy: copy.wait())

    used = meta[blocks]
    per = sub // s
    subs = group // per

    def rows(k):
        return pl.ds(k * sub, sub)

    def query(k):
        return q_ref[k * per : (k + 1) * per].reshape(sub, q_ref.shape[2])

    first = (1 + root) * BLOCK
    k0 = keys[:, :first]
    v0 = keys[:lat, :first]
    row = lax.broadcasted_iota(jnp.int32, (s, first), 0)
    col = lax.broadcasted_iota(jnp.int32, (s, first), 1)
    own = jnp.where((col <= row) | (col >= s), bias[:, :first], HIDDEN)
    for k in range(subs):
        raw = jnp.dot(query(k), k0, preferred_element_type=jnp.float32)
        sc = (raw.reshape(per, s, first) + own[None]).reshape(sub, first)
        m = jnp.max(sc, axis=1, keepdims=True)
        p = jnp.exp2((sc - m) * factor)
        m_ref[rows(k), :] = jnp.broadcast_to(m, (sub, 128))
        l_ref[rows(k), :] = lane_sums(p)
        acc_ref[rows(k), :] = lax.dot_general(
            p.astype(jnp.bfloat16), v0, NT, preferred_element_type=jnp.float32
        )

    def chunk(lane, size):
        lane = pl.multiple_of(lane, BLOCK)
        kk = keys[:, pl.ds(lane, size)]
        vv = keys[:lat, pl.ds(lane, size)]
        hide = bias[:, pl.ds(lane, size)]
        for k in range(subs):
            sc = jnp.dot(query(k), kk, preferred_element_type=jnp.float32) + hide
            old = m_ref[rows(k), :]
            m = jnp.maximum(old, jnp.max(sc, axis=1, keepdims=True))
            fade = jnp.exp2((old - m) * factor)
            p = jnp.exp2((sc - jnp.tile(m, (1, size // 128))) * factor)
            m_ref[rows(k), :] = m
            l_ref[rows(k), :] = l_ref[rows(k), :] * fade + lane_sums(p)
            acc_ref[rows(k), :] = acc_ref[rows(k), :] * jnp.tile(
                fade, (1, lat // 128)
            ) + lax.dot_general(
                p.astype(jnp.bfloat16), vv, NT, preferred_element_type=jnp.float32
            )

    left = used - (1 + root)
    many = left // wide

    def big(i, carry):
        chunk(first + i * (wide * BLOCK), wide * BLOCK)
        return carry

    lax.fori_loop(0, many, big, 0)
    at = first + many * (wide * BLOCK)
    rem = left - many * wide
    size = wide // 2
    while size:
        take = rem >= size

        @pl.when(take)
        def _(at=at, size=size):
            chunk(at, size * BLOCK)

        at = at + jnp.where(take, size * BLOCK, 0)
        rem = rem - jnp.where(take, size, 0)
        size //= 2

    for g in range(group):
        r = pl.ds(g * s, s)
        total = jnp.sum(l_ref[r, :], axis=1, keepdims=True)
        o = (acc_ref[r, :] * (1.0 / total)).astype(jnp.bfloat16)
        out_ref[:, g * vd : (g + 1) * vd] = jnp.dot(
            o, wuv_ref[g], preferred_element_type=jnp.float32
        ).astype(jnp.bfloat16)


def attend(counts, owners, query, seg_t, seen, w_uv, pieces, scale, group=8, sub=1024, wide=4):
    heads, s, depth = query.shape
    lat, vd = w_uv.shape[1:]
    trunk = seen.shape[1]
    group = min(group, heads)
    sub = min(sub, group * s)
    total = group * s
    return pl.pallas_call(
        functools.partial(
            attend_kernel, pieces=len(pieces), sub=sub, wide=wide, scale=scale
        ),
        grid_spec=pltpu.PrefetchScalarGridSpec(
            num_scalar_prefetch=2,
            grid=(heads // group,),
            in_specs=[
                pl.BlockSpec((group, s, depth), lambda i, *_: (i, 0, 0)),
                pl.BlockSpec((depth, s), lambda i, *_: (0, 0)),
                pl.BlockSpec((1, trunk), lambda i, *_: (0, 0)),
                pl.BlockSpec((group, lat, vd), lambda i, *_: (i, 0, 0)),
            ]
            + [pl.BlockSpec(memory_space=pl.ANY)] * len(pieces),
            out_specs=pl.BlockSpec((s, group * vd), lambda i, *_: (0, i)),
            scratch_shapes=[
                pltpu.VMEM((depth, trunk + BLOCK), jnp.bfloat16),
                pltpu.VMEM((1, trunk + BLOCK), jnp.float32),
                pltpu.VMEM((total, 128), jnp.float32),
                pltpu.VMEM((total, 128), jnp.float32),
                pltpu.VMEM((total, lat), jnp.float32),
                pltpu.SMEM((trunk // BLOCK + 1,), jnp.int32),
                pltpu.SemaphoreType.DMA,
            ],
        ),
        out_shape=jax.ShapeDtypeStruct((s, heads * vd), jnp.bfloat16),
        compiler_params=pltpu.CompilerParams(vmem_limit_bytes=56 << 20),
        cost_estimate=pl.CostEstimate(
            flops=2 * heads * s * (trunk // 2) * (depth + lat),
            bytes_accessed=2 * (query.size + w_uv.size + trunk * depth),
            transcendentals=heads * s * trunk // 2,
        ),
        name="attend",
    )(counts, owners, query, seg_t, seen, w_uv, *pieces)


def gather_trunk(trunk, branches, heads):
    devices = branches * heads
    me = lax.axis_index("branch") * heads + lax.axis_index("head")
    if trunk.shape[0] != BLOCK or branches != 8 or heads != 4:
        whole = lax.all_gather(trunk, AXES, axis=0, tiled=True)
        return [whole.T[None]], jnp.arange(whole.shape[0] // BLOCK, dtype=jnp.int32)

    def send(x, by_core):
        pairs = [(i, i ^ by_core[i & 1]) for i in range(devices)]
        return lax.ppermute(x, AXES, pairs)

    mine = trunk.T[None]
    column = jnp.concatenate([mine] + [send(mine, (8 * d, 8 * d)) for d in (1, 2, 3)], axis=0)
    side = send(column, (2, 4))
    both = jnp.concatenate([column, side], axis=0)
    cross = send(both, (4, 2))
    here = [both, cross]
    there = [send(both, (1, 1)), send(cross, (1, 1))]
    core = me & 1
    one, two = 2 + 2 * core, 4 - 2 * core
    steps = jnp.arange(4, dtype=jnp.int32) * 8
    mine_of = lambda one, two: jnp.concatenate(
        [steps, steps ^ one, steps ^ two, steps ^ one ^ two]
    )
    owners = jnp.concatenate([me ^ mine_of(one, two), me ^ 1 ^ mine_of(two, one)])
    return here + there, owners


def make_shards(branches, heads):
    def shards(q_latent, seg_latent, trunk_latent, visible, w_uq, w_uk, w_uv):
        heads_here, nope, lat = w_uk.shape
        rope = w_uq.shape[1] // heads_here - nope
        half = rope // 2
        scale = 1.0 / (nope + rope) ** 0.5
        rank = q_latent.shape[1]
        joined = lax.all_gather(
            jnp.concatenate([q_latent, seg_latent], axis=1), "head", axis=0, tiled=True
        )
        pieces, owners = gather_trunk(trunk_latent, branches, heads)
        seg_len = joined.shape[0]
        counts = jnp.sum(visible.reshape(-1, BLOCK), axis=1)
        position = (jnp.sum(visible) + jnp.arange(seg_len, dtype=jnp.int32)).astype(jnp.float32)
        freq = 10000.0 ** (-2.0 * jnp.arange(half, dtype=jnp.float32) / rope)
        angle = position[:, None] * freq[None, :]
        cosine = jnp.cos(angle)
        sine = jnp.sin(angle)
        query = make_query(
            joined,
            jnp.concatenate([cosine, cosine], axis=1),
            jnp.concatenate([-sine, sine], axis=1),
            w_uq,
            w_uk,
        )
        return attend(
            counts, owners, query, joined[:, rank:].T, visible, w_uv, pieces, scale
        )

    return shards


def solution(mesh):
    placed = (
        P(("branch", "head"), None),
        P(("branch", "head"), None),
        P(("branch", "head"), None),
        P("branch", None),
        P(None, "head"),
        P("head", None, None),
        P("head", None, None),
    )
    return jax.shard_map(
        make_shards(mesh.shape["branch"], mesh.shape["head"]),
        mesh=mesh,
        in_specs=placed,
        out_specs=P("branch", "head"),
        check_vma=False,
    )
```

time: 252 us -> 111 us (0.44)
  matrix products: 129 us -> 0 us
  Pallas kernels: 0 us -> 57.7 us
  local copies, waits for them, and re-layouts: 41.6 us -> 6.91 us
  other arithmetic: 36.1 us -> 4.11 us
  between operations: 13.5 us -> 0.18 us
  starting transfers between devices: 0.01 us -> 5.52 us
  blocking collectives: 12.7 us -> 16.4 us
  waiting for transfers between devices: 15.1 us -> 17.9 us
    dot_general x21 -> x0, matrix products: 129 us -> none  [the longest x9 57.1 us: absorb(): jnp.einsum('shk,kc->shc', weights.astype(jnp.bfloat16), keys[:, :summed_o...]
    pallas_call x0 -> x2, Pallas kernels: none -> 57.7 us  [the longest x1 49 us: attend(): pl.pallas_call(functools.partial(attend_kernel, pieces=len(pieces), sub=s...]
    while x57 -> x0, local copies, waits for them, and re-layouts: 33.3 us -> none
    reduce_sum x10 -> x2, other arithmetic: 21.1 us -> 1.31 us  [the longest x1 0.67 us: shards(): jnp.sum(visible) + jnp.arange(seg_len, dtype=jnp.int32)]
    ppermute x0 -> x7, waiting for transfers between devices: none -> 17.9 us  [send(): return lax.ppermute(x, AXES, pairs)]
    all_gather x1 -> x0, waiting for transfers between devices: 14.4 us -> none  [shards(): lax.all_gather(trunk_latent, ('branch', 'head'), axis=0, tiled=True)]
    gt x8 -> x0, other arithmetic: 7.3 us -> none  [take_piece(): marks = lax.dynamic_slice_in_dim(seen, start, piece.shape[0], 0) > 0]
    ppermute x0 -> x7, starting transfers between devices: none -> 5.52 us  [send(): return lax.ppermute(x, AXES, pairs)]
  transfers between devices with their start and end apart: 1 -> 7, of which waited for: 1 -> 3; matrix products, arithmetic and copies ran while one was open for 18% -> 4% of each run, Pallas kernels for 0% -> 8%
where the time goes in v1:
time: 111 us; the launch traced here: 109 us
  Pallas kernels  57.7 us (52%)
  waiting for transfers between devices  17.9 us (16%)
  blocking collectives  16.4 us (15%)
  local copies, waits for them, and re-layouts  6.91 us (6%)
  starting transfers between devices  5.52 us (5%)
  other arithmetic  4.11 us (4%)
    pallas_call x1, Pallas kernels, attend(): pl.pallas_call(functools.partial(attend_kernel, pieces=len(pieces), sub=s...  49 us
    ppermute x7, waiting for transfers between devices, send(): return lax.ppermute(x, AXES, pairs)  17.9 us
    all_gather x1, blocking collectives, shards(): lax.all_gather(jnp.concatenate([q_latent, seg_latent], axis=1), 'head', a...  16.4 us
    pallas_call x1, Pallas kernels, make_query(): pl.pallas_call(functools.partial(query_kernel, rope=rope), grid=(heads //...  8.78 us
    unnamed x25, local copies, waits for them, and re-layouts  6.82 us
    ppermute x7, starting transfers between devices, send(): return lax.ppermute(x, AXES, pairs)  5.52 us
  transfers between devices with their start and end apart: 7, of which 3 were waited for; matrix products, arithmetic and copies ran while one was open for 4% of the time, Pallas kernels for 8%

profile of v1, /device:TPU:21, one launch (start us, length us, event | category | flops | bytes accessed | tf_op | source)
XLA Modules:
  0.0 108.8 jit_solution(17874844614415726752)
XLA Ops:
  0.0 0.0 copy-start.2
  0.0 0.2 collective-permute-start.2
  0.2 3.2 %collective-permute-start.1 = (bf16[1,576,128]{2,1,0:T(8,128)(2,1)}, bf16[1,576,128]{2,1,0:T(8,128)(2,1)S(1)}, u32[]{:S(2)}, u32[]{:S(2)}) collective-permute-start(bf16[1,576,128]{2,1,0:T(8,128)(2,1)} %bitcast.7), channel_id=1, source_target_pairs={{0,16},{1,17},{2,18},{3,19},{4,20},{5,21},{6,22},{7,23},{8,24},{9,... | collective-permute-start | bytes 442376 | tf_op jit(solution)/shard_map/ppermute | solution.py:250
  3.4 0.0 collective-permute-start
  3.4 5.8 %collective-permute-done.2 = bf16[1,576,128]{2,1,0:T(8,128)(2,1)S(1)} collective-permute-done((bf16[1,576,128]{2,1,0:T(8,128)(2,1)}, bf16[1,576,128]{2,1,0:T(8,128)(2,1)S(1)}, u32[]{:S(2)}, u32[]{:S(2)}) %collective-permute-start.2) | collective-permute-done | bytes 147488 | tf_op jit(solution)/shard_map/ppermute | solution.py:250
  9.1 3.5 %collective-permute-done.1 = bf16[1,576,128]{2,1,0:T(8,128)(2,1)S(1)} collective-permute-done((bf16[1,576,128]{2,1,0:T(8,128)(2,1)}, bf16[1,576,128]{2,1,0:T(8,128)(2,1)S(1)}, u32[]{:S(2)}, u32[]{:S(2)}) %collective-permute-start.1) | collective-permute-done | bytes 147488 | tf_op jit(solution)/shard_map/ppermute | solution.py:250
  12.6 0.0 collective-permute-done
  12.6 1.0 pad_maximum_fusion
  13.6 0.0 copy-start.4
  13.6 0.0 copy-start.3
  13.6 0.0 copy-start.5
  13.6 0.3 collective-permute-start.3
  13.9 0.0 copy-done.2
  14.0 8.7 %collective-permute-done.3 = bf16[4,576,128]{2,1,0:T(8,128)(2,1)S(1)} collective-permute-done((bf16[4,576,128]{2,1,0:T(8,128)(2,1)S(1)}, bf16[4,576,128]{2,1,0:T(8,128)(2,1)S(1)}, u32[]{:S(2)}, u32[]{:S(2)}) %collective-permute-start.3) | collective-permute-done | bytes 589856 | tf_op jit(solution)/shard_map/ppermute | solution.py:250
  22.7 0.1 constant_dynamic-update-slice_fusion.rest_0_
  22.8 0.0 copy-start.6
  22.8 1.3 %collective-permute-start.4 = (bf16[8,576,128]{2,1,0:T(8,128)(2,1)S(1)}, bf16[8,576,128]{2,1,0:T(8,128)(2,1)S(1)}, u32[]{:S(2)}, u32[]{:S(2)}) collective-permute-start(bf16[8,576,128]{2,1,0:T(8,128)(2,1)S(1)} %constant_dynamic-update-slice_fusion.rest_0_), channel_id=1, source_target_pairs={{0,4},{1,3},{2,6},{3,1},{4,0},{5,7},{6,2},{7,5},{8,12},{9,11},{10,... | collective-permute-start | bytes 3538952 | tf_op jit(solution)/shard_map/ppermute | solution.py:250
  24.1 0.0 copy-done.4
  24.1 0.7 reduce_sum.19
  24.8 0.6 reduce_sum.18.counts
  25.4 0.0 copy-done.3
  25.4 0.0 copy-done.5
  25.4 16.4 %all_gather.3.qs_ref = bf16[128,2112]{1,0:T(8,128)(2,1)S(1)} all-gather(bf16[32,2112]{1,0:T(8,128)(2,1)S(1)} %pad_maximum_fusion.1), channel_id=1, replica_groups=mesh['branch'=8,'head'=4] {'head'}, dimensions={0}, use_global_device_ids=true | all-gather | bytes 675840 | tf_op jit(solution)/shard_map/all_gather | solution.py:276
  41.9 0.8 copy.14
  42.7 0.4 collective-permute-start.5
  43.1 0.0 collective-permute-done.4.rest_1_
  43.1 0.0 copy-start.7
  43.1 0.2 collective-permute-start.6
  43.2 0.7 add_convert_fusion
  44.0 0.1 add_xor_fusion
  44.0 0.6 pad_add_fusion.owners
  44.6 0.3 fusion
  45.0 0.1 pad_maximum_fusion.2
  45.1 0.0 copy-start.1
  45.1 2.2 %copy-done.1 = bf16[32,128,512]{2,1,0:T(8,128)(2,1)S(1)} copy-done((bf16[32,128,512]{2,1,0:T(8,128)(2,1)S(1)}, bf16[32,128,512]{2,1,0:T(8,128)(2,1)}, u32[]{:S(2)}) %copy-start.1) | copy-done | bytes 4194328
  47.3 8.8 %query.1.q_ref = bf16[32,128,576]{2,1,0:T(8,128)(2,1)S(1)} custom-call(bf16[128,2112]{1,0:T(8,128)(2,1)S(1)} %all_gather.3.qs_ref, f32[128,64]{1,0:T(8,128)S(1)} %get-tuple-element.14.cos_ref, f32[128,64]{1,0:T(8,128)S(1)} %get-tuple-element.15.sin_ref, bf16[1536,6144]{1,0:T(8,128)(2,1)} %wuq_ref.1, bf16[32,128,512]{2,1,0:T(8,128)(2,1)S(1)} %copy-done.1), custom_call_target="tpu_custom_call" | custom-call | flops 2952790016 | bytes 27787264 | tf_op jit(solution)/shard_map/query/pallas_call | solution.py:39
  56.0 0.0 copy-done.6
  56.1 0.0 copy-done.7
  56.1 0.0 copy-start
  56.1 2.3 %copy-done = bf16[32,128,576]{2,1,0:T(8,128)(2,1)} copy-done((bf16[32,128,576]{2,1,0:T(8,128)(2,1)}, bf16[32,128,576]{2,1,0:T(8,128)(2,1)S(1)}, u32[]{:S(2)}) %copy-start) | copy-done | bytes 4718616
  58.4 0.0 collective-permute-done.5.rest_2_
  58.4 0.0 copy-start.8
  58.4 0.0 collective-permute-done.6.rest_3_
  58.4 0.0 copy-start.9
  58.4 1.1 %copy-done.8 = bf16[8,576,128]{2,1,0:T(8,128)(2,1)} copy-done((bf16[8,576,128]{2,1,0:T(8,128)(2,1)}, bf16[8,576,128]{2,1,0:T(8,128)(2,1)S(1)}, u32[]{:S(2)}) %copy-start.8) | copy-done | bytes 1179672
  59.5 0.3 copy-done.9
  59.8 49.0 %attend.1 = bf16[128,4096]{1,0:T(8,128)(2,1)} custom-call(s32[32]{0:T(128)} %reduce_sum.18.counts, s32[32]{0:T(128)} %pad_add_fusion.owners, bf16[32,128,576]{2,1,0:T(8,128)(2,1)} %copy-done, bf16[576,128]{1,0:T(8,128)(2,1)} %bitcast.10, s32[1,4096]{1,0:T(1,128)} %seen_ref.1, bf16[32,512,128]{2,1,0:T(8,128)(2,1)} %wuv_ref.1, bf16[8,576,128]{2,1,0:T(8,128)(2,1)} %copy-done.6, ...), custom_call_target="tpu_custom_call" | custom-call | flops 18253611008 | bytes 13631488 | tf_op jit(solution)/shard_map/attend/pallas_call | solution.py:205
  (10 shorter events, 0.1 us)
Async XLA Ops:
  0.0 13.9 %copy-start.2 = (bf16[128,576]{0,1:T(8,128)(2,1)S(1)}, bf16[128,576]{0,1:T(8,128)(2,1)}, u32[]{:S(2)}) copy-start(bf16[128,576]{0,1:T(8,128)(2,1)} %param.9) | copy-start | bytes 442372
  0.0 9.1 %collective-permute-start.2 = (bf16[1,576,128]{2,1,0:T(8,128)(2,1)}, bf16[1,576,128]{2,1,0:T(8,128)(2,1)S(1)}, u32[]{:S(2)}, u32[]{:S(2)}) collective-permute-start(bf16[1,576,128]{2,1,0:T(8,128)(2,1)} %bitcast.6), channel_id=1, source_target_pairs={{0,24},{1,25},{2,26},{3,27},{4,28},{5,29},{6,30},{7,31},{8,16},{9,... | collective-permute-start | bytes 442376 | tf_op jit(solution)/shard_map/ppermute | solution.py:250
  0.2 12.4 %collective-permute-start.1 = (bf16[1,576,128]{2,1,0:T(8,128)(2,1)}, bf16[1,576,128]{2,1,0:T(8,128)(2,1)S(1)}, u32[]{:S(2)}, u32[]{:S(2)}) collective-permute-start(bf16[1,576,128]{2,1,0:T(8,128)(2,1)} %bitcast.7), channel_id=1, source_target_pairs={{0,16},{1,17},{2,18},{3,19},{4,20},{5,21},{6,22},{7,23},{8,24},{9,... | collective-permute-start | bytes 442376 | tf_op jit(solution)/shard_map/ppermute | solution.py:250
  3.4 9.2 %collective-permute-start = (bf16[1,576,128]{2,1,0:T(8,128)(2,1)}, bf16[1,576,128]{2,1,0:T(8,128)(2,1)S(1)}, u32[]{:S(2)}, u32[]{:S(2)}) collective-permute-start(bf16[1,576,128]{2,1,0:T(8,128)(2,1)} %bitcast.8), channel_id=1, source_target_pairs={{0,8},{1,9},{2,10},{3,11},{4,12},{5,13},{6,14},{7,15},{8,0},{9,1},... | collective-permute-start | bytes 442376 | tf_op jit(solution)/shard_map/ppermute | solution.py:250
  13.6 10.5 %copy-start.4 = (s32[1,4096]{1,0:T(1,128)S(1)}, s32[1,4096]{1,0:T(1,128)}, u32[]{:S(2)}) copy-start(s32[1,4096]{1,0:T(1,128)} %seen_ref.1) | copy-start | bytes 49156
  13.6 11.8 %copy-start.3 = (bf16[32,1536]{1,0:T(8,128)(2,1)S(1)}, bf16[32,1536]{1,0:T(8,128)(2,1)}, u32[]{:S(2)}) copy-start(bf16[32,1536]{1,0:T(8,128)(2,1)} %param.7) | copy-start | bytes 294916
  13.6 11.8 %copy-start.5 = (bf16[32,576]{1,0:T(8,128)(2,1)S(1)}, bf16[32,576]{1,0:T(8,128)(2,1)}, u32[]{:S(2)}) copy-start(bf16[32,576]{1,0:T(8,128)(2,1)} %param.8) | copy-start | bytes 110596
  13.6 9.1 %collective-permute-start.3 = (bf16[4,576,128]{2,1,0:T(8,128)(2,1)S(1)}, bf16[4,576,128]{2,1,0:T(8,128)(2,1)S(1)}, u32[]{:S(2)}, u32[]{:S(2)}) collective-permute-start(bf16[4,576,128]{2,1,0:T(8,128)(2,1)S(1)} %pad_maximum_fusion), channel_id=1, source_target_pairs={{0,2},{1,5},{2,0},{3,7},{4,6},{5,1},{6,4},{7,3},{8,10},{9,13},{10,... | collective-permute-start | bytes 1769480 | tf_op jit(solution)/shard_map/ppermute | solution.py:250
  22.8 33.2 %copy-start.6 = (bf16[8,576,128]{2,1,0:T(8,128)(2,1)}, bf16[8,576,128]{2,1,0:T(8,128)(2,1)S(1)}, u32[]{:S(2)}) copy-start(bf16[8,576,128]{2,1,0:T(8,128)(2,1)S(1)} %constant_dynamic-update-slice_fusion.rest_0_) | copy-start | bytes 3538948
  22.8 20.3 %collective-permute-start.4 = (bf16[8,576,128]{2,1,0:T(8,128)(2,1)S(1)}, bf16[8,576,128]{2,1,0:T(8,128)(2,1)S(1)}, u32[]{:S(2)}, u32[]{:S(2)}) collective-permute-start(bf16[8,576,128]{2,1,0:T(8,128)(2,1)S(1)} %constant_dynamic-update-slice_fusion.rest_0_), channel_id=1, source_target_pairs={{0,4},{1,3},{2,6},{3,1},{4,0},{5,7},{6,2},{7,5},{8,12},{9,11},{10,... | collective-permute-start | bytes 3538952 | tf_op jit(solution)/shard_map/ppermute | solution.py:250
  42.7 15.7 %collective-permute-start.5 = (bf16[8,576,128]{2,1,0:T(8,128)(2,1)S(1)}, bf16[8,576,128]{2,1,0:T(8,128)(2,1)S(1)}, u32[]{:S(2)}, u32[]{:S(2)}) collective-permute-start(bf16[8,576,128]{2,1,0:T(8,128)(2,1)S(1)} %constant_dynamic-update-slice_fusion.rest_0_), channel_id=1, source_target_pairs={{0,1},{1,0},{2,3},{3,2},{4,5},{5,4},{6,7},{7,6},{8,9},{9,8},{10,11... | collective-permute-start | bytes 3538952 | tf_op jit(solution)/shard_map/ppermute | solution.py:250
  43.1 13.0 %copy-start.7 = (bf16[8,576,128]{2,1,0:T(8,128)(2,1)}, bf16[8,576,128]{2,1,0:T(8,128)(2,1)S(1)}, u32[]{:S(2)}) copy-start(bf16[8,576,128]{2,1,0:T(8,128)(2,1)S(1)} %collective-permute-done.4.rest_1_) | copy-start | bytes 3538948
  43.1 15.3 %collective-permute-start.6 = (bf16[8,576,128]{2,1,0:T(8,128)(2,1)S(1)}, bf16[8,576,128]{2,1,0:T(8,128)(2,1)S(1)}, u32[]{:S(2)}, u32[]{:S(2)}) collective-permute-start(bf16[8,576,128]{2,1,0:T(8,128)(2,1)S(1)} %collective-permute-done.4.rest_1_), channel_id=1, source_target_pairs={{0,1},{1,0},{2,3},{3,2},{4,5},{5,4},{6,7},{7,6},{8,9},{9,8},{10,11... | collective-permute-start | bytes 3538952 | tf_op jit(solution)/shard_map/ppermute | solution.py:250
  45.1 2.2 %copy-start.1 = (bf16[32,128,512]{2,1,0:T(8,128)(2,1)S(1)}, bf16[32,128,512]{2,1,0:T(8,128)(2,1)}, u32[]{:S(2)}) copy-start(bf16[32,128,512]{2,1,0:T(8,128)(2,1)} %wuk_ref.1) | copy-start | bytes 12582916
  56.1 2.3 %copy-start = (bf16[32,128,576]{2,1,0:T(8,128)(2,1)}, bf16[32,128,576]{2,1,0:T(8,128)(2,1)S(1)}, u32[]{:S(2)}) copy-start(bf16[32,128,576]{2,1,0:T(8,128)(2,1)S(1)} %query.1.q_ref) | copy-start | bytes 14155780
  58.4 1.1 %copy-start.8 = (bf16[8,576,128]{2,1,0:T(8,128)(2,1)}, bf16[8,576,128]{2,1,0:T(8,128)(2,1)S(1)}, u32[]{:S(2)}) copy-start(bf16[8,576,128]{2,1,0:T(8,128)(2,1)S(1)} %collective-permute-done.5.rest_2_) | copy-start | bytes 3538948
  58.4 1.5 %copy-start.9 = (bf16[8,576,128]{2,1,0:T(8,128)(2,1)}, bf16[8,576,128]{2,1,0:T(8,128)(2,1)S(1)}, u32[]{:S(2)}) copy-start(bf16[8,576,128]{2,1,0:T(8,128)(2,1)S(1)} %collective-permute-done.6.rest_3_) | copy-start | bytes 3538948
